TPU v7x, 128 devices: a whole 4x4x4 slice. The times are simulated.
128 devices in a mesh: row: 8 (over z, y_lo), col: 16 (over y_hi, x, core).
Axes of the slice: x: 4, y: 4 (y_hi: 2, y_lo: 2; y = y_hi * 2 + y_lo), z: 4, core: 2. Of those that a mesh axis runs over, the one named last changes fastest.
Arguments:
- fock: bfloat16 [4096, 65536], P('row', 'col'), may hold values from -6 to 6
- pattern: int32 [64, 1024], P('row', 'col'), may hold values 0 or 1
- coeffs: bfloat16 [65536, 4096], P('col', 'row'), may hold values from -0.0390625 to 0.0390625
- order: int32 [64], replicated, may hold values from 0 to 63, as said below
Outputs:
- band_step: float32 [2, 2048, 4096], P(None, 'row', 'col')
Inputs may be any that keep to these rules, and one draw needn't show every extreme that they name: `order`: a permutation of the atom blocks; the block at position p, with s = p mod (8), lies in a row tile t (t = block div (4)) with t mod 8 = s div (1).
All inputs are finite; a program needn't handle non-finite values. No bound on the sum of `pattern` on one device may be relied on, other than what follows from the above.
Results may differ from a plain program's by a relative error of at most 0.0003.
Values may be sent and summed in bfloat16 or wider, within the bound.
No kernel may reach another device: no remote copies, remote signals or barrier semaphores. Data moves between devices by JAX's collectives and lax.ppermute only.
A program may use at most 128 MiB of HBM per device.

v0:
```python
import jax
import jax.numpy as jnp
from jax import lax
from jax.sharding import PartitionSpec as P

BLK = 64
NB = 256


HIGHEST_PRECISION = lax.Precision.HIGHEST


def from_root(value, axis, source):
    kept = jnp.where(lax.axis_index(axis) == source, value, 0).astype(value.dtype)
    return lax.psum(kept, axis)


def orthonormal(tall_matrix):
    gram_matrix = lax.psum(jnp.dot(tall_matrix.T, tall_matrix, precision=HIGHEST_PRECISION), "row")
    lower_factor = jnp.linalg.cholesky(gram_matrix)
    return jax.scipy.linalg.solve_triangular(lower_factor, tall_matrix.T, lower=True).T


def body(fock, pattern, coeffs, order):
    grid_count = lax.axis_size("row")
    here_row = lax.axis_index("row")
    here_col = lax.axis_index("col")
    rows_here = fock.shape[0]
    col_blocks = pattern.shape[1]
    occupied = pattern.astype(jnp.bfloat16)[:, None, :, None]
    masked = (fock.reshape(rows_here // BLK, BLK, col_blocks, BLK) * occupied).reshape(fock.shape)
    partials = jnp.dot(
        masked,
        lax.all_gather(coeffs, "row", axis=1, tiled=True),
        preferred_element_type=jnp.float32,
    )
    reduced = lax.psum_scatter(partials, "col", scatter_dimension=1, tiled=True)
    col_width = reduced.shape[1]
    slot_count = rows_here // BLK
    per_pair = slot_count // grid_count
    tile_blocks = NB // BLK
    received = lax.all_to_all(
        reduced.reshape(grid_count, per_pair * BLK, col_width),
        "row",
        split_axis=0,
        concat_axis=0,
        tiled=True,
    )
    arrived = lax.dynamic_slice_in_dim(
        order.reshape(grid_count, grid_count, per_pair), here_row, 1, 1
    ).reshape(slot_count)
    target = arrived // (tile_blocks * grid_count) * tile_blocks + arrived % tile_blocks
    slot_ids = jnp.arange(slot_count, dtype=jnp.int32)
    matches = (target[None, :] == slot_ids[:, None]).astype(jnp.int32)
    source = jnp.sum(matches * slot_ids[None, :], axis=1)
    elpa_rows = jnp.take(received, source, axis=0).reshape(rows_here, col_width)
    cycles = rows_here // NB
    row_index = jnp.arange(rows_here, dtype=jnp.int32)
    global_row = (row_index // NB * grid_count + here_row) * NB + row_index % NB
    trailing = (global_row >= NB).astype(jnp.float32)[:, None]
    reflector = orthonormal(orthonormal(elpa_rows * trailing))
    reflector = from_root(reflector, "col", 0)
    gathered = lax.all_gather(reflector, "row", axis=0, tiled=True)
    arranged = (
        gathered.reshape(grid_count, cycles, NB, NB)
        .transpose(1, 0, 2, 3)
        .reshape(grid_count * rows_here, NB)
    )
    col_basis = lax.dynamic_slice_in_dim(arranged, here_col * col_width, col_width, 0)
    image_part = jnp.dot(elpa_rows, col_basis, precision=HIGHEST_PRECISION)
    left_part = jnp.dot(reflector.T, elpa_rows, precision=HIGHEST_PRECISION)
    image_cols = lax.psum(image_part, "col")
    left_rows = lax.psum(left_part, "row")
    core_block = lax.psum(jnp.dot(reflector.T, image_cols, precision=HIGHEST_PRECISION), "row")
    updated = (
        elpa_rows
        - 2.0 * jnp.dot(reflector, left_rows, precision=HIGHEST_PRECISION)
        - 2.0 * jnp.dot(image_cols, col_basis.T, precision=HIGHEST_PRECISION)
        + 4.0
        * jnp.dot(
            reflector,
            jnp.dot(core_block, col_basis.T, precision=HIGHEST_PRECISION),
            precision=HIGHEST_PRECISION,
        )
    )
    return updated.reshape(cycles, NB, col_width)


def solution(mesh):
    return jax.shard_map(
        body,
        mesh=mesh,
        in_specs=(P("row", "col"), P("row", "col"), P("col", "row"), P()),
        out_specs=P(None, "row", "col"),
        check_vma=False,
    )
```

profile of v0, /device:TPU:0, one launch (start us, length us, event | category | flops | bytes accessed | tf_op | source)
XLA Modules:
  0.0 1551.4 jit_solution(688840702138272161)
XLA Ops:
  6.5 0.7 all-gather.3.cloned.1.call-update
  7.3 5.4 mul.79
  12.7 12.2 mul.80
  24.9 626.8 %all-gather.3.cloned.1.call-done = bf16[4096,4096]{1,0:T(8,128)(2,1)} async-done(((bf16[4096,512]{1,0:T(8,128)(2,1)}), bf16[4096,4096]{1,0:T(8,128)(2,1)}) %all-gather.3.cloned.1.call-update) | async-done | bytes 33554448 | tf_op jit(solution)/shard_map/all_gather | solution.py:34
  651.7 25.1 %fusion = f32[512,4096]{1,0:T(8,128)} fusion(bf16[4096,4096]{1,0:T(8,128)(2,1)} %all-gather.3.cloned.1.call-done, bf16[512,4096]{1,0:T(8,128)(2,1)} %param.7, bf16[512,4096]{1,0:T(8,128)(2,1)} %mul.80), kind=kOutput, calls=%fused_computation.5 | convolution fusion | flops 17181966336 | bytes 50331648 | tf_op jit(solution)/shard_map/dot_general | solution.py:32
  677.9 102.7 %reduce-scatter.2.cloned.1.call-done = f32[512,256]{1,0:T(8,128)} async-done(((f32[512,4096]{1,0:T(8,128)}), f32[512,256]{1,0:T(8,128)}) %reduce-scatter.2.cloned.1.call-update) | async-done | bytes 524304 | tf_op jit(solution)/shard_map/reduce_scatter | solution.py:37
  780.7 4.5 all-to-all-start
  785.2 8.9 all-to-all-done
  794.7 1.9 convolution_bitcast_fusion
  797.3 70.8 %all-reduce.8.cloned.1.call-done = f32[256,256]{0,1:T(8,128)} async-done(((f32[256,256]{0,1:T(8,128)}), f32[256,256]{0,1:T(8,128)}) %all-reduce.8.cloned.1.call-update) | async-done | bytes 262160 | tf_op jit(solution)/shard_map/psum | solution.py:19
  868.1 1.1 copy.26
  869.2 1.0 fusion.19
  870.2 11.7 cholesky.130
  882.0 9.8 custom-call.13
  892.2 11.7 cholesky.147
  904.0 0.7 compare_reduce_fusion.2
  906.2 4.3 while.4
  907.0 1.4 bitcast_dynamic-update-slice_fusion.4
  909.1 1.4 bitcast_dynamic-update-slice_fusion.4
  910.5 19.7 %custom-call.14 = f32[2,128,128]{1,2,0:T(8,128)S(1)} custom-call(f32[2,128,128]{2,1,0:T(8,128)S(1)} %get-tuple-element.21), custom_call_target="InvertDiagBlocksLowerTriangular" | custom-call | tf_op jit(solution)/shard_map/jit(_solve_triangular)/triangular_solve | solution.py:21
  931.4 1.3 fusion.5
  932.8 73.4 %all-reduce.10.cloned.1.call-done = f32[256,256]{0,1:T(8,128)} async-done(((f32[256,256]{0,1:T(8,128)}), f32[256,256]{0,1:T(8,128)}) %all-reduce.10.cloned.1.call-update) | async-done | bytes 262160 | tf_op jit(solution)/shard_map/psum | solution.py:19
  1006.2 1.1 copy.28
  1007.3 1.0 fusion.18
  1008.3 11.7 cholesky.164
  1020.1 9.8 custom-call.15
  1030.4 11.7 cholesky.181
  1042.1 0.6 compare_reduce_fusion.1
  1042.8 0.7 compare_reduce_fusion
  1044.9 4.4 while.5
  1045.7 1.4 bitcast_dynamic-update-slice_fusion.5
  1047.8 1.4 bitcast_dynamic-update-slice_fusion.5
  1049.2 19.7 %custom-call.16 = f32[2,128,128]{1,2,0:T(8,128)S(1)} custom-call(f32[2,128,128]{2,1,0:T(8,128)S(1)} %get-tuple-element.22), custom_call_target="InvertDiagBlocksLowerTriangular" | custom-call | tf_op jit(solution)/shard_map/jit(_solve_triangular)/triangular_solve | solution.py:21
  1070.2 0.8 fusion.9
  1071.1 137.8 %all-reduce.12.cloned.1.call-done = f32[512,256]{0,1:T(8,128)} async-done(((f32[512,256]{0,1:T(8,128)}), f32[512,256]{0,1:T(8,128)}) %all-reduce.12.cloned.1.call-update) | async-done | bytes 524304 | tf_op jit(solution)/shard_map/psum | solution.py:15
  1209.0 93.6 %all-gather.5.cloned.1.call-done = f32[4096,256]{0,1:T(8,128)} async-done(((f32[512,256]{0,1:T(8,128)}), f32[4096,256]{0,1:T(8,128)}) %all-gather.5.cloned.1.call-update) | async-done | bytes 4194320 | tf_op jit(solution)/shard_map/all_gather | solution.py:63
  1302.6 6.6 reshape.163
  1309.2 7.3 copy.30
  1316.5 2.7 fusion.12
  1319.3 1.3 fusion.14
  1320.6 137.1 %all-reduce.14.cloned.1.call-done = f32[512,256]{1,0:T(8,128)} async-done(((f32[512,256]{1,0:T(8,128)}), f32[512,256]{1,0:T(8,128)}) %all-reduce.14.cloned.1.call-update) | async-done | bytes 524304 | tf_op jit(solution)/shard_map/psum | solution.py:72
  1457.8 2.4 fusion.81
  1460.2 77.5 %all-reduce.16.cloned.1.call-done = (f32[256,256]{1,0:T(8,128)}, f32[256,256]{1,0:T(8,128)}) async-done(((f32[256,256]{1,0:T(8,128)}, f32[256,256]{1,0:T(8,128)}), (f32[256,256]{1,0:T(8,128)}, f32[256,256]{1,0:T(8,128)})) %all-reduce.16.cloned.1.call-update) | async-done | bytes 524304 | tf_op jit(solution)/shard_map/psum | solution.py:73
  1537.7 1.4 fusion.27
  1539.2 1.6 fusion.4
  1540.8 1.6 fusion.3
  1542.4 0.7 fusion.2
  1543.1 1.0 copy.40
  (70 shorter events, 8.8 us)
Async XLA Ops:
  6.5 0.8 copy-start.2
  6.5 645.2 %all-gather.3.cloned.1.call-start = ((), (), s32[]{:S(2)}) async-start(), calls=%async_computation.2 | async-start | bytes 37748736 | tf_op jit(solution)/shard_map/all_gather | solution.py:34
  7.3 773.4 %reduce-scatter.2.cloned.1.call-start = ((), (), s32[]{:S(2)}) async-start(), calls=%async_computation.3 | async-start | bytes 8912896 | tf_op jit(solution)/shard_map/reduce_scatter | solution.py:37
  676.9 0.7 copy-start.3
  780.7 13.4 all-to-all-start
  785.1 83.0 %all-reduce.8.cloned.1.call-start = ((), (), s32[]{:S(2)}) async-start(), calls=%async_computation.4 | async-start | bytes 524288 | tf_op jit(solution)/shard_map/psum | solution.py:19
  796.6 209.6 %all-reduce.10.cloned.1.call-start = ((), (), s32[]{:S(2)}) async-start(), calls=%async_computation.5 | async-start | bytes 524288 | tf_op jit(solution)/shard_map/psum | solution.py:19
  932.8 276.1 %all-reduce.12.cloned.1.call-start = ((), (), s32[]{:S(2)}) async-start(), calls=%async_computation.6 | async-start | bytes 1048576 | tf_op jit(solution)/shard_map/psum | solution.py:15
  1071.0 231.6 %all-gather.5.cloned.1.call-start = ((), (), s32[]{:S(2)}) async-start(), calls=%async_computation.7 | async-start | bytes 4718592 | tf_op jit(solution)/shard_map/all_gather | solution.py:63
  1208.9 248.9 %all-reduce.14.cloned.1.call-start = ((), (), s32[]{:S(2)}) async-start(), calls=%async_computation.8 | async-start | bytes 1048576 | tf_op jit(solution)/shard_map/psum | solution.py:72
  1309.2 10.1 copy-start
  1319.3 218.5 %all-reduce.16.cloned.1.call-start = ((), (), s32[]{:S(2)}) async-start(), calls=%async_computation.9 | async-start | bytes 1048576 | tf_op jit(solution)/shard_map/psum | solution.py:73
  1457.8 83.0 %copy-start.1 = (f32[512,256]{1,0:T(8,128)S(1)}, f32[512,256]{1,0:T(8,128)}, u32[]{:S(2)}) copy-start(f32[512,256]{1,0:T(8,128)} %all-reduce.14.cloned.1.call-done) | copy-start | bytes 1572868
Sparse Core Ops, SparseCore 0:
  9.0 642.6 all-gather.2
  677.0 103.6 reduce-scatter.1
  796.7 71.3 all-reduce.7
  932.9 73.2 all-reduce.9
  1071.1 137.6 all-reduce.11
  1210.5 92.0 all-gather.4
  1319.4 138.3 all-reduce.13
  1460.3 77.3 all-reduce.15
where the time goes:
time: 1560 us; the launch traced here: 1550 us
  waiting for transfers between devices  1330 us (85%)
  other arithmetic  111 us (7%)
  local copies, waits for them, and re-layouts  44.7 us (3%)
  matrix products  43.6 us (3%)
  between operations  16.9 us (1%)
    all_gather x1, waiting for transfers between devices, body(): lax.all_gather(coeffs, 'row', axis=1, tiled=True)  627 us
    psum x2, waiting for transfers between devices, orthonormal(): lax.psum(jnp.dot(tall_matrix.T, tall_matrix, precision=HIGHEST_PRECISION)...  144 us
    psum x1, waiting for transfers between devices, from_root(): return lax.psum(kept, axis)  138 us
    psum x1, waiting for transfers between devices, body(): image_cols = lax.psum(image_part, 'col')  137 us
    reduce_scatter x1, waiting for transfers between devices, body(): reduced = lax.psum_scatter(partials, 'col', scatter_dimension=1, tiled=True)  103 us
    all_gather x1, waiting for transfers between devices, body(): gathered = lax.all_gather(reflector, 'row', axis=0, tiled=True)  93.6 us
    psum x1, waiting for transfers between devices, body(): left_rows = lax.psum(left_part, 'row')  77.5 us
    another operation x13, other arithmetic, orthonormal(): lower_factor = jnp.linalg.cholesky(gram_matrix)  68.7 us
  transfers between devices with their start and end apart: 9, of which 9 were waited for; matrix products, arithmetic and copies ran while one was open for 1% of the time, Pallas kernels for 0%

commit v1 on v0

v1 whole, which is shorter than its diff:
```python
import jax
import jax.numpy as jnp
from jax import lax
from jax.sharding import PartitionSpec as P

BLK = 64
NB = 256
AXES = ("row", "col")
HIGHEST_PRECISION = lax.Precision.HIGHEST


def locate(index):
    row, col = divmod(index, 16)
    z, y_lo = divmod(row, 2)
    y_hi, rest = divmod(col, 8)
    x, core = divmod(rest, 2)
    return x, y_hi * 2 + y_lo, z, core


def index_of(x, y, z, core):
    y_hi, y_lo = divmod(y, 2)
    return (z % 4 * 2 + y_lo) * 16 + y_hi * 8 + x % 4 * 2 + core


def moves(step, only=lambda x, y, z, core: True):
    return [(i, index_of(*step(*locate(i)))) for i in range(128) if only(*locate(i))]


MOVES = {
    "core": moves(lambda x, y, z, core: (x, y, z, 1 - core)),
    "y_lo": moves(lambda x, y, z, core: (x, y ^ 1, z, core)),
    "y_hi": moves(lambda x, y, z, core: (x, y ^ 2, z, core)),
    "z_up": moves(lambda x, y, z, core: (x, y, z + 1, core)),
    "z_down": moves(lambda x, y, z, core: (x, y, z + 3, core)),
    "z_far": moves(lambda x, y, z, core: (x, y, z + 2, core)),
    "z_a": moves(lambda x, y, z, core: (x, y, z ^ 1, core)),
    "z_b": moves(lambda x, y, z, core: (x, y, z ^ 3, core)),
    "x_a": moves(lambda x, y, z, core: (x ^ 1, y, z, core)),
    "x_b": moves(lambda x, y, z, core: (x ^ 3, y, z, core)),
    "turn": moves(
        lambda x, y, z, core: (z, y, x, core),
        lambda x, y, z, core: core == y % 2,
    ),
}


def deal(high, low):
    def step(x, y, z, core):
        return (z // 2 ^ high) * 2 + y % 2, y // 2 * 2 + core, x, z % 2 ^ low
    return moves(step)


def send(value, move):
    return lax.ppermute(value, AXES, MOVES[move] if isinstance(move, str) else move)


def pick(value, index, axis=0):
    return lax.dynamic_index_in_dim(value, index, axis, keepdims=False)


def total(value, *steps):
    for step in steps:
        value = value + send(value, step)
    return value


def mm(a, b):
    return jnp.dot(a, b, precision=HIGHEST_PRECISION)


def inverse_factor(gram):
    lower = jnp.linalg.cholesky(gram)
    return jax.scipy.linalg.solve_triangular(lower, jnp.eye(NB, dtype=jnp.float32), lower=True).T


def body(fock, pattern, coeffs, order):
    row = lax.axis_index("row")
    col = lax.axis_index("col")
    z, y_lo = row // 2, row % 2
    y_hi, x, core = col // 8, col // 2 % 4, col % 2
    depth = fock.shape[1]

    spread = (jnp.arange(depth)[None, :] // BLK == jnp.arange(depth // BLK)[:, None]).astype(jnp.bfloat16)
    occupied = jnp.dot(pattern.astype(jnp.bfloat16), spread).astype(jnp.bfloat16)
    fock = fock.reshape(4, 2, BLK, depth)
    occupied = occupied.reshape(4, 2, 1, depth)

    def masked_half(which):
        return (pick(fock, which, 1) * pick(occupied, which, 1)).reshape(4 * BLK, depth)

    own = jnp.concatenate([masked_half(1 - core), masked_half(core)], axis=0)
    peer = send(own, "y_lo")
    rows_given = jnp.concatenate([own[: 4 * BLK], peer[: 4 * BLK]], axis=0)
    rows_kept = jnp.concatenate([own[4 * BLK :], peer[4 * BLK :]], axis=0)

    def gather_columns(part):
        above = send(part, "z_down")
        below = send(part, "z_up")
        far_top = send(above[: depth // 2], "z_down")
        far_bottom = send(below[depth // 2 :], "z_up")
        far = jnp.concatenate([far_top, far_bottom], axis=0)
        return jnp.concatenate([part, above, far, below], axis=1)

    def product(columns):
        given = jnp.dot(rows_given, columns, preferred_element_type=jnp.float32)
        kept = jnp.dot(rows_kept, columns, preferred_element_type=jnp.float32)
        return (kept + send(given, "core")).reshape(2, 4, BLK, 4, NB)

    def pair(value, first, second):
        return jnp.stack([pick(value, first), pick(value, second)])

    def reduce_columns(part):
        one, two = part[0], part[1]
        one = pair(one, x, x ^ 3) + send(pair(one, x ^ 1, x ^ 2), "x_a")
        two = pair(two, x, x ^ 1) + send(pair(two, x ^ 3, x ^ 2), "x_b")
        one = one[0] + send(one[1], "x_b")
        two = two[0] + send(two[1], "x_a")
        both = jnp.stack([one, two])

        def side(which):
            return jnp.stack([pick(both, (2 * which + i - z) % 4, 2) for i in range(2)], axis=2)

        return side(y_hi) + send(side(1 - y_hi), "y_hi")

    parts = []
    for j in range(2):
        parts.append(reduce_columns(product(gather_columns(coeffs[:, j * NB : (j + 1) * NB]))))

    order = order.reshape(8, 8)
    piece = parts[0][:, :, 0, :]
    piece = jnp.where(y_hi == 0, piece, send(piece, "y_hi"))
    piece = jnp.where(y_lo == 0, piece, send(piece, "y_lo"))
    atoms_here = pick(order, 2 * x + core, 1)
    piece_atoms = lax.dynamic_slice_in_dim(atoms_here, 2 * z, 2, 0)
    piece = piece * (piece_atoms >= NB // BLK).astype(jnp.float32)[:, None, None]
    flat = piece.reshape(2 * BLK, NB)
    plane = ("core", "x_a", "x_b", "z_a", "z_b")
    first = inverse_factor(total(mm(flat.T, flat), *plane))
    flat = mm(flat, first)
    second = inverse_factor(total(mm(flat.T, flat), *plane))
    factor = mm(first, second)

    slots = jnp.arange(8, dtype=jnp.int32)

    def source_of_slot(atoms):
        target = atoms // 32 * 4 + atoms % 4
        return jnp.sum((target[None, :] == slots[:, None]).astype(jnp.int32) * slots[None, :], axis=1)

    ring = jnp.stack([piece, send(piece, "z_down"), send(piece, "z_far"), send(piece, "z_up")]).reshape(8, BLK, NB)
    source = source_of_slot(atoms_here)
    tiles = jnp.take(ring, (source // 2 - z) % 4 * 2 + source % 2, axis=0).reshape(2, NB, NB)
    panel_cols = pick(tiles, y_hi)
    panel_rows = send(tiles.reshape(2 * NB, NB), "turn")
    panel_rows = jnp.where(core == y_lo, panel_rows, send(panel_rows, "core"))

    both = jnp.stack(parts)
    arrived = []
    for high in range(2):
        for low in range(2):
            chosen = pick(pick(both, z % 2 ^ low), z // 2 ^ high, 2)
            arrived.append(send(chosen, deal(high, low)))
    arrived = jnp.stack(arrived).reshape(8, BLK, NB)
    source = source_of_slot(pick(order, row, 1))
    z_from, y_from = source // 2, source % 2
    turn = ((x // 2) ^ (z_from // 2)) * 2 + (core ^ (z_from % 2))
    matrix = jnp.take(arrived, turn * 2 + (y_from ^ (x % 2)), axis=0).reshape(2 * NB, NB)

    left = total(mm(panel_rows.T, matrix), "z_a", "z_b", "y_lo")
    image = total(mm(matrix, panel_cols), "core", "x_a", "x_b", "y_hi")
    centre = total(mm(panel_rows.T, image), "z_a", "z_b", "y_lo")

    left = mm(factor.T, left)
    image = mm(image, factor)
    centre = mm(mm(factor.T, centre), factor)
    basis_rows = mm(panel_rows, factor)
    basis_cols = mm(panel_cols, factor)
    updated = (
        matrix
        - 2.0 * mm(basis_rows, left - mm(centre, basis_cols.T))
        - 2.0 * mm(image - mm(basis_rows, centre), basis_cols.T)
    )
    return updated.reshape(2, NB, NB)


def solution(mesh):
    return jax.shard_map(
        body,
        mesh=mesh,
        in_specs=(P("row", "col"), P("row", "col"), P("col", "row"), P()),
        out_specs=P(None, "row", "col"),
        check_vma=False,
    )
```

time: 1560 us -> 517 us (0.33)
  waiting for transfers between devices: 1330 us -> 195 us
  starting transfers between devices: 4.91 us -> 77.2 us
  matrix products: 43.6 us -> 65.9 us
  other arithmetic: 111 us -> 129 us
    all_gather x2 -> x0, waiting for transfers between devices: 720 us -> none  [the longest x1 627 us: body(): lax.all_gather(coeffs, 'row', axis=1, tiled=True)]
    psum x5 -> x0, waiting for transfers between devices: 497 us -> none  [the longest x2 144 us: orthonormal(): lax.psum(jnp.dot(tall_matrix.T, tall_matrix, precision=HIGHEST_PRECISION)...]
    ppermute x0 -> x52, waiting for transfers between devices: none -> 195 us  [send(): lax.ppermute(value, AXES, MOVES[move] if isinstance(move, str) else move)]
    reduce_scatter x1 -> x0, waiting for transfers between devices: 103 us -> none  [body(): reduced = lax.psum_scatter(partials, 'col', scatter_dimension=1, tiled=True)]
    ppermute x0 -> x52, starting transfers between devices: none -> 77.2 us  [send(): lax.ppermute(value, AXES, MOVES[move] if isinstance(move, str) else move)]
    dot_general x10 -> x22, matrix products: 40.2 us -> 60.9 us  [the longest x2 24.3 us: product(): given = jnp.dot(rows_given, columns, preferred_element_type=jnp.float32)]
    mul x2 -> x0, local copies, waits for them, and re-layouts: 17.6 us -> none  [body(): fock.reshape(rows_here // BLK, BLK, col_blocks, BLK) * occupied]
    another operation x18 -> x35, other arithmetic: 108 us -> 114 us  [the longest x14 69.9 us: inverse_factor(): lower = jnp.linalg.cholesky(gram)]
  transfers between devices with their start and end apart: 9 -> 52, of which waited for: 9 -> 27; matrix products, arithmetic and copies ran while one was open for 1% -> 43% of each run, Pallas kernels for 0% -> 0%
where the time goes in v1:
time: 517 us; the launch traced here: 509 us
  waiting for transfers between devices  195 us (38%)
  other arithmetic  129 us (25%)
  starting transfers between devices  77.2 us (15%)
  matrix products  65.9 us (13%)
  local copies, waits for them, and re-layouts  37.5 us (7%)
    ppermute x52, waiting for transfers between devices, send(): lax.ppermute(value, AXES, MOVES[move] if isinstance(move, str) else move)  195 us
    ppermute x52, starting transfers between devices, send(): lax.ppermute(value, AXES, MOVES[move] if isinstance(move, str) else move)  77.2 us
    another operation x14, other arithmetic, inverse_factor(): lower = jnp.linalg.cholesky(gram)  69.9 us
    another operation x5, other arithmetic, inverse_factor(): jax.scipy.linalg.solve_triangular(lower, jnp.eye(NB, dtype=jnp.float32),...  41.2 us
    dot_general x2, matrix products, product(): given = jnp.dot(rows_given, columns, preferred_element_type=jnp.float32)  24.3 us
    dot_general x2, matrix products, product(): kept = jnp.dot(rows_kept, columns, preferred_element_type=jnp.float32)  24 us
    dot_general x17, matrix products, mm(): return jnp.dot(a, b, precision=HIGHEST_PRECISION)  11.6 us
  transfers between devices with their start and end apart: 52, of which 27 were waited for; matrix products, arithmetic and copies ran while one was open for 43% of the time, Pallas kernels for 0%

profile of v1, /device:TPU:0, one launch (start us, length us, event | category | flops | bytes accessed | tf_op | source)
XLA Modules:
  0.0 508.9 jit_solution(4613975520667521666)
XLA Ops:
  1.0 2.7 constant_dynamic-slice_fusion.23
  11.7 4.0 collective-permute-start.1
  15.8 3.2 collective-permute-start.11
  19.4 42.8 %collective-permute-done.1 = bf16[4096,256]{1,0:T(8,128)(2,1)} collective-permute-done((bf16[4096,256]{1,0:T(8,128)(2,1)}, bf16[4096,256]{1,0:T(8,128)(2,1)}, u32[]{:S(2)}, u32[]{:S(2)}) %collective-permute-start.1) | collective-permute-done | bytes 2097184 | tf_op jit(solution)/shard_map/ppermute | solution.py:54
  63.4 3.8 collective-permute-start.2
  68.6 38.5 %collective-permute-done.11 = bf16[4096,256]{1,0:T(8,128)(2,1)} collective-permute-done((bf16[4096,256]{1,0:T(8,128)(2,1)}, bf16[4096,256]{1,0:T(8,128)(2,1)}, u32[]{:S(2)}, u32[]{:S(2)}) %collective-permute-start.11) | collective-permute-done | bytes 2097184 | tf_op jit(solution)/shard_map/ppermute | solution.py:54
  108.4 3.8 collective-permute-start.12
  113.5 2.8 fusion.95
  116.4 13.0 %collective-permute-done.2 = bf16[2048,256]{1,0:T(8,128)(2,1)S(1)} collective-permute-done((bf16[2048,256]{1,0:T(8,128)(2,1)S(1)}, bf16[2048,256]{1,0:T(8,128)(2,1)S(1)}, u32[]{:S(2)}, u32[]{:S(2)}) %collective-permute-start.2) | collective-permute-done | bytes 1048608 | tf_op jit(solution)/shard_map/ppermute | solution.py:54
  129.5 3.7 collective-permute-done.4
  134.1 8.8 %fusion.3 = f32[512,1024]{1,0:T(8,128)} fusion(bf16[256,4096]{1,0:T(8,128)(2,1)S(1)} %copy-done.1, bf16[256,4096]{1,0:T(8,128)(2,1)S(1)} %get-tuple-element.53, bf16[4096,256]{1,0:T(8,128)(2,1)} %collective-permute-done.3, bf16[2048,256]{1,0:T(8,128)(2,1)} %copy-done.14, bf16[2048,256]{1,0:T(8,128)(2,1)} %copy-done.13, ...), kind=kOutput, calls=%fused_computation.15 | convolution fusion | flops 4345298944 | bytes 14680064 | tf_op jit(solution)/shard_map/dot_general | solution.py:105
  143.2 7.3 %collective-permute-done.12 = bf16[2048,256]{1,0:T(8,128)(2,1)S(1)} collective-permute-done((bf16[2048,256]{1,0:T(8,128)(2,1)S(1)}, bf16[2048,256]{1,0:T(8,128)(2,1)S(1)}, u32[]{:S(2)}, u32[]{:S(2)}) %collective-permute-start.12) | collective-permute-done | bytes 1048608 | tf_op jit(solution)/shard_map/ppermute | solution.py:54
  150.5 3.5 collective-permute-done.14
  154.0 15.5 %fusion.2 = f32[512,1024]{1,0:T(8,128)} fusion(bf16[256,4096]{1,0:T(8,128)(2,1)S(1)} %copy-done.1, bf16[256,4096]{1,0:T(8,128)(2,1)S(1)} %get-tuple-element.53, bf16[4096,256]{1,0:T(8,128)(2,1)} %collective-permute-done.13, bf16[2048,256]{1,0:T(8,128)(2,1)} %collective-permute-done.14, bf16[2048,256]{1,0:T(8,128)(2,1)S(1)} %collective-permute-done.12, ...), kind=kOutput, calls=%fused_computation.14 | convolution fusion | flops 4345298944 | bytes 14680064 | tf_op jit(solution)/shard_map/dot_general | solution.py:105
  169.7 8.6 %fusion.4 = f32[512,1024]{1,0:T(8,128)S(1)} fusion(f32[512,1024]{1,0:T(8,128)} %collective-permute-done.5, bf16[256,4096]{1,0:T(8,128)(2,1)S(1)} %get-tuple-element.52, bf16[256,4096]{1,0:T(8,128)(2,1)S(1)} %get-tuple-element.105, bf16[4096,256]{1,0:T(8,128)(2,1)} %collective-permute-done.3, bf16[2048,256]{1,0:T(8,128)(2,1)} %copy-done.14, ...), kind=kOutput, calls=%fused_computation.18 | convolution fusion | flops 4345823232 | bytes 16777216 | tf_op jit(solution)/shard_map/dot_general | solution.py:106
  182.8 2.8 collective-permute-start.8
  190.9 15.4 %fusion.5 = f32[512,1024]{1,0:T(8,128)S(1)} fusion(f32[512,1024]{1,0:T(8,128)} %collective-permute-done.15, bf16[256,4096]{1,0:T(8,128)(2,1)S(1)} %copy-done.4, bf16[256,4096]{1,0:T(8,128)(2,1)S(1)} %get-tuple-element.105, bf16[4096,256]{1,0:T(8,128)(2,1)} %collective-permute-done.13, bf16[2048,256]{1,0:T(8,128)(2,1)} %collective-permute-done.14, ...), kind=kOutput, calls=%fused_computation.19 | convolution fusion | flops 4345823232 | bytes 16777216 | tf_op jit(solution)/shard_map/dot_general | solution.py:106
  217.2 7.2 %collective-permute-done.18 = f32[2,64,4,256]{3,1,2,0:T(8,128)} collective-permute-done((f32[2,64,4,256]{3,1,2,0:T(8,128)}, f32[2,64,4,256]{3,1,2,0:T(8,128)}, u32[]{:S(2)}, u32[]{:S(2)}) %collective-permute-start.18) | collective-permute-done | bytes 524320 | tf_op jit(solution)/shard_map/ppermute | solution.py:54
  227.6 3.3 collective-permute-done.9
  231.1 3.3 collective-permute-start.10
  235.4 3.3 collective-permute-start.20
  239.9 3.3 collective-permute-start.25
  243.2 2.9 collective-permute-done.20
  246.9 3.2 collective-permute-start.22
  250.1 7.7 %collective-permute-start.23 = (f32[2,64,256]{2,1,0:T(8,128)S(1)}, f32[2,64,256]{2,1,0:T(8,128)S(1)}, u32[]{:S(2)}, u32[]{:S(2)}) collective-permute-start(f32[2,64,256]{2,1,0:T(8,128)S(1)} %get-tuple-element.79), channel_id=1, source_target_pairs={{0,4},{1,20},{2,36},{3,52},{4,68},{5,84},{6,100},{7,116},{8,12},{9... | collective-permute-start | bytes 393224 | tf_op jit(solution)/shard_map/ppermute | solution.py:54
  258.2 3.4 collective-permute-done.23
  264.7 6.5 %collective-permute-start.27 = (f32[2,64,256]{2,1,0:T(8,128)S(1)}, f32[2,64,256]{2,1,0:T(8,128)S(1)}, u32[]{:S(2)}, u32[]{:S(2)}) collective-permute-start(f32[2,64,256]{2,1,0:T(8,128)S(1)} %select_multiply_fusion), channel_id=1, source_target_pairs={{0,96},{1,97},{2,98},{3,99},{4,100},{5,101},{6,102},{7,103},{8,104... | collective-permute-start | bytes 393224 | tf_op jit(solution)/shard_map/ppermute | solution.py:54
  272.9 4.0 collective-permute-done.27
  281.9 8.7 %collective-permute-done.33 = f32[256,256]{0,1:T(8,128)S(1)} collective-permute-done((f32[256,256]{0,1:T(8,128)S(1)}, f32[256,256]{0,1:T(8,128)S(1)}, u32[]{:S(2)}, u32[]{:S(2)}) %collective-permute-start.33) | collective-permute-done | bytes 262176 | tf_op jit(solution)/shard_map/ppermute | solution.py:54
  294.5 6.0 %collective-permute-done.34 = f32[256,256]{0,1:T(8,128)S(1)} collective-permute-done((f32[256,256]{0,1:T(8,128)S(1)}, f32[256,256]{0,1:T(8,128)S(1)}, u32[]{:S(2)}, u32[]{:S(2)}) %collective-permute-start.34) | collective-permute-done | bytes 262176 | tf_op jit(solution)/shard_map/ppermute | solution.py:54
  300.7 12.6 %collective-permute-done.35 = f32[256,256]{0,1:T(8,128)S(1)} collective-permute-done((f32[256,256]{0,1:T(8,128)S(1)}, f32[256,256]{0,1:T(8,128)S(1)}, u32[]{:S(2)}, u32[]{:S(2)}) %collective-permute-start.35) | collective-permute-done | bytes 262176 | tf_op jit(solution)/shard_map/ppermute | solution.py:54
  314.7 4.0 collective-permute-start.47
  318.7 4.1 collective-permute-done.36
  323.1 11.7 %cholesky.130 = f32[128,128]{1,0:T(8,128)S(1)} custom-call(f32[128,128]{1,0:T(8,128)S(1)} %cholesky.194), custom_call_target="Cholesky" | custom-call | tf_op jit(solution)/shard_map/jit(cholesky)/cholesky | solution.py:72
  334.8 9.8 %custom-call.13 = f32[1,128,128]{1,2,0:T(8,128)S(1)} custom-call(f32[1,128,128]{2,1,0:T(8,128)S(1)} %get-tuple-element.95), custom_call_target="InvertDiagBlocksLowerTriangular" | custom-call | tf_op jit(solution)/shard_map/jit(cholesky)/cholesky | solution.py:72
  345.1 11.7 %cholesky.147 = f32[128,128]{1,0:T(8,128)S(1)} custom-call(f32[128,128]{1,0:T(8,128)S(1)} %slice_subtract_fusion.1), custom_call_target="Cholesky" | custom-call | tf_op jit(solution)/shard_map/jit(cholesky)/cholesky | solution.py:72
  359.7 4.4 while.4
  364.1 19.7 %custom-call.14 = f32[2,128,128]{1,2,0:T(8,128)S(1)} custom-call(f32[2,128,128]{2,1,0:T(8,128)S(1)} %get-tuple-element.22), custom_call_target="InvertDiagBlocksLowerTriangular" | custom-call | tf_op jit(solution)/shard_map/jit(_solve_triangular)/triangular_solve | solution.py:73
  390.6 3.4 collective-permute-start.48
  396.4 7.5 %collective-permute-done.42 = f32[256,256]{1,0:T(8,128)S(1)} collective-permute-done((f32[256,256]{1,0:T(8,128)S(1)}, f32[256,256]{1,0:T(8,128)S(1)}, u32[]{:S(2)}, u32[]{:S(2)}) %collective-permute-start.42) | collective-permute-done | bytes 262176 | tf_op jit(solution)/shard_map/ppermute | solution.py:54
  408.5 6.1 %collective-permute-done.40 = f32[256,256]{0,1:T(8,128)S(1)} collective-permute-done((f32[256,256]{0,1:T(8,128)S(1)}, f32[256,256]{0,1:T(8,128)S(1)}, u32[]{:S(2)}, u32[]{:S(2)}) %collective-permute-start.40) | collective-permute-done | bytes 262176 | tf_op jit(solution)/shard_map/ppermute | solution.py:54
  420.5 3.6 collective-permute-done.41
  426.7 11.7 %cholesky.164 = f32[128,128]{1,0:T(8,128)S(1)} custom-call(f32[128,128]{1,0:T(8,128)S(1)} %cholesky.197), custom_call_target="Cholesky" | custom-call | tf_op jit(solution)/shard_map/jit(cholesky)/cholesky | solution.py:72
  439.2 9.8 %custom-call.15 = f32[1,128,128]{1,2,0:T(8,128)S(1)} custom-call(f32[1,128,128]{2,1,0:T(8,128)S(1)} %get-tuple-element.91), custom_call_target="InvertDiagBlocksLowerTriangular" | custom-call | tf_op jit(solution)/shard_map/jit(cholesky)/cholesky | solution.py:72
  451.8 11.7 %cholesky.181 = f32[128,128]{1,0:T(8,128)S(1)} custom-call(f32[128,128]{1,0:T(8,128)S(1)} %slice_subtract_fusion), custom_call_target="Cholesky" | custom-call | tf_op jit(solution)/shard_map/jit(cholesky)/cholesky | solution.py:72
  467.8 4.2 while.5
  472.6 20.5 %custom-call.16 = f32[2,128,128]{1,2,0:T(8,128)S(1)} custom-call(f32[2,128,128]{2,1,0:T(8,128)} %copy-done.9), custom_call_target="InvertDiagBlocksLowerTriangular" | custom-call | tf_op jit(solution)/shard_map/jit(_solve_triangular)/triangular_solve | solution.py:73
  496.8 5.4 %collective-permute-done.51 = f32[256,256]{1,0:T(8,128)S(1)} collective-permute-done((f32[256,256]{1,0:T(8,128)S(1)}, f32[256,256]{1,0:T(8,128)S(1)}, u32[]{:S(2)}, u32[]{:S(2)}) %collective-permute-start.51) | collective-permute-done | bytes 262176 | tf_op jit(solution)/shard_map/ppermute | solution.py:54
  (264 shorter events, 107.6 us)
Async XLA Ops:
  7.8 105.7 %collective-permute-start = (bf16[512,4096]{1,0:T(8,128)(2,1)}, bf16[512,4096]{1,0:T(8,128)(2,1)}, u32[]{:S(2)}, u32[]{:S(2)}) collective-permute-start(bf16[512,4096]{1,0:T(8,128)(2,1)} %pad_maximum_fusion.3), channel_id=1, source_target_pairs={{0,16},{1,17},{2,18},{3,19},{4,20},{5,21},{6,22},{7,23},{8,24},{9,... | collective-permute-start | bytes 12582920 | tf_op jit(solution)/shard_map/ppermute | solution.py:54
  11.7 50.4 %collective-permute-start.1 = (bf16[4096,256]{1,0:T(8,128)(2,1)}, bf16[4096,256]{1,0:T(8,128)(2,1)}, u32[]{:S(2)}, u32[]{:S(2)}) collective-permute-start(bf16[4096,256]{1,0:T(8,128)(2,1)} %get-tuple-element.51), channel_id=1, source_target_pairs={{0,96},{1,97},{2,98},{3,99},{4,100},{5,101},{6,102},{7,103},{8,104... | collective-permute-start | bytes 6291464 | tf_op jit(solution)/shard_map/ppermute | solution.py:54
  15.8 51.4 %collective-permute-start.3 = (bf16[4096,256]{1,0:T(8,128)(2,1)}, bf16[4096,256]{1,0:T(8,128)(2,1)}, u32[]{:S(2)}, u32[]{:S(2)}) collective-permute-start(bf16[4096,256]{1,0:T(8,128)(2,1)} %get-tuple-element.51), channel_id=1, source_target_pairs={{0,32},{1,33},{2,34},{3,35},{4,36},{5,37},{6,38},{7,39},{8,40},{9,... | collective-permute-start | bytes 6291464 | tf_op jit(solution)/shard_map/ppermute | solution.py:54
  15.8 91.3 %collective-permute-start.11 = (bf16[4096,256]{1,0:T(8,128)(2,1)}, bf16[4096,256]{1,0:T(8,128)(2,1)}, u32[]{:S(2)}, u32[]{:S(2)}) collective-permute-start(bf16[4096,256]{1,0:T(8,128)(2,1)} %get-tuple-element.50), channel_id=1, source_target_pairs={{0,96},{1,97},{2,98},{3,99},{4,100},{5,101},{6,102},{7,103},{8,104... | collective-permute-start | bytes 6291464 | tf_op jit(solution)/shard_map/ppermute | solution.py:54
  19.0 93.2 %collective-permute-start.13 = (bf16[4096,256]{1,0:T(8,128)(2,1)}, bf16[4096,256]{1,0:T(8,128)(2,1)}, u32[]{:S(2)}, u32[]{:S(2)}) collective-permute-start(bf16[4096,256]{1,0:T(8,128)(2,1)} %get-tuple-element.50), channel_id=1, source_target_pairs={{0,32},{1,33},{2,34},{3,35},{4,36},{5,37},{6,38},{7,39},{8,40},{9,... | collective-permute-start | bytes 6291464 | tf_op jit(solution)/shard_map/ppermute | solution.py:54
  63.4 66.0 %collective-permute-start.2 = (bf16[2048,256]{1,0:T(8,128)(2,1)S(1)}, bf16[2048,256]{1,0:T(8,128)(2,1)S(1)}, u32[]{:S(2)}, u32[]{:S(2)}) collective-permute-start(bf16[2048,256]{1,0:T(8,128)(2,1)S(1)} %slice.139), channel_id=1, source_target_pairs={{0,96},{1,97},{2,98},{3,99},{4,100},{5,101},{6,102},{7,103},{8,104... | collective-permute-start | bytes 3145736 | tf_op jit(solution)/shard_map/ppermute | solution.py:54
  68.5 64.7 %collective-permute-start.4 = (bf16[2048,256]{1,0:T(8,128)(2,1)S(1)}, bf16[2048,256]{1,0:T(8,128)(2,1)S(1)}, u32[]{:S(2)}, u32[]{:S(2)}) collective-permute-start(bf16[2048,256]{1,0:T(8,128)(2,1)S(1)} %slice.140), channel_id=1, source_target_pairs={{0,32},{1,33},{2,34},{3,35},{4,36},{5,37},{6,38},{7,39},{8,40},{9,... | collective-permute-start | bytes 3145736 | tf_op jit(solution)/shard_map/ppermute | solution.py:54
  108.4 42.1 %collective-permute-start.12 = (bf16[2048,256]{1,0:T(8,128)(2,1)S(1)}, bf16[2048,256]{1,0:T(8,128)(2,1)S(1)}, u32[]{:S(2)}, u32[]{:S(2)}) collective-permute-start(bf16[2048,256]{1,0:T(8,128)(2,1)S(1)} %slice.148), channel_id=1, source_target_pairs={{0,96},{1,97},{2,98},{3,99},{4,100},{5,101},{6,102},{7,103},{8,104... | collective-permute-start | bytes 3145736 | tf_op jit(solution)/shard_map/ppermute | solution.py:54
  113.4 40.5 %collective-permute-start.14 = (bf16[2048,256]{1,0:T(8,128)(2,1)S(1)}, bf16[2048,256]{1,0:T(8,128)(2,1)}, u32[]{:S(2)}, u32[]{:S(2)}) collective-permute-start(bf16[2048,256]{1,0:T(8,128)(2,1)S(1)} %slice.149), channel_id=1, source_target_pairs={{0,32},{1,33},{2,34},{3,35},{4,36},{5,37},{6,38},{7,39},{8,40},{9,... | collective-permute-start | bytes 3145736 | tf_op jit(solution)/shard_map/ppermute | solution.py:54
  142.9 26.7 %collective-permute-start.5 = (f32[512,1024]{1,0:T(8,128)}, f32[512,1024]{1,0:T(8,128)}, u32[]{:S(2)}, u32[]{:S(2)}) collective-permute-start(f32[512,1024]{1,0:T(8,128)} %fusion.3), channel_id=1, source_target_pairs={{0,1},{1,0},{2,3},{3,2},{4,5},{5,4},{6,7},{7,6},{8,9},{9,8},{10,11... | collective-permute-start | bytes 6291464 | tf_op jit(solution)/shard_map/ppermute | solution.py:54
  169.5 21.4 %collective-permute-start.15 = (f32[512,1024]{1,0:T(8,128)}, f32[512,1024]{1,0:T(8,128)}, u32[]{:S(2)}, u32[]{:S(2)}) collective-permute-start(f32[512,1024]{1,0:T(8,128)} %fusion.2), channel_id=1, source_target_pairs={{0,1},{1,0},{2,3},{3,2},{4,5},{5,4},{6,7},{7,6},{8,9},{9,8},{10,11... | collective-permute-start | bytes 6291464 | tf_op jit(solution)/shard_map/ppermute | solution.py:54
  182.8 28.5 %collective-permute-start.8 = (f32[2,64,4,256]{3,1,2,0:T(8,128)}, f32[2,64,4,256]{3,1,2,0:T(8,128)}, u32[]{:S(2)}, u32[]{:S(2)}) collective-permute-start(f32[2,64,4,256]{3,1,2,0:T(8,128)} %pad_maximum_fusion.14), channel_id=1, source_target_pairs={{0,6},{1,7},{2,4},{3,5},{4,2},{5,3},{6,0},{7,1},{8,14},{9,15},{10,... | collective-permute-start | bytes 1572872 | tf_op jit(solution)/shard_map/ppermute | solution.py:54
  190.6 23.2 %collective-permute-start.6 = (f32[2,64,4,256]{3,1,2,0:T(8,128)}, f32[2,64,4,256]{3,1,2,0:T(8,128)}, u32[]{:S(2)}, u32[]{:S(2)}) collective-permute-start(f32[2,64,4,256]{3,1,2,0:T(8,128)} %pad_maximum_fusion.13), channel_id=1, source_target_pairs={{0,2},{1,3},{2,0},{3,1},{4,6},{5,7},{6,4},{7,5},{8,10},{9,11},{10,... | collective-permute-start | bytes 1572872 | tf_op jit(solution)/shard_map/ppermute | solution.py:54
  208.1 16.3 %collective-permute-start.18 = (f32[2,64,4,256]{3,1,2,0:T(8,128)}, f32[2,64,4,256]{3,1,2,0:T(8,128)}, u32[]{:S(2)}, u32[]{:S(2)}) collective-permute-start(f32[2,64,4,256]{3,1,2,0:T(8,128)} %pad_maximum_fusion.16), channel_id=1, source_target_pairs={{0,6},{1,7},{2,4},{3,5},{4,2},{5,3},{6,0},{7,1},{8,14},{9,15},{10,... | collective-permute-start | bytes 1572872 | tf_op jit(solution)/shard_map/ppermute | solution.py:54
  210.4 15.9 %collective-permute-start.16 = (f32[2,64,4,256]{3,1,2,0:T(8,128)S(1)}, f32[2,64,4,256]{3,1,2,0:T(8,128)S(1)}, u32[]{:S(2)}, u32[]{:S(2)}) collective-permute-start(f32[2,64,4,256]{3,1,2,0:T(8,128)S(1)} %pad_maximum_fusion.15), channel_id=1, source_target_pairs={{0,2},{1,3},{2,0},{3,1},{4,6},{5,7},{6,4},{7,5},{8,10},{9,11},{10,... | collective-permute-start | bytes 1572872 | tf_op jit(solution)/shard_map/ppermute | solution.py:54
  212.4 18.5 %collective-permute-start.9 = (f32[64,4,256]{2,0,1:T(8,128)S(1)}, f32[64,4,256]{2,0,1:T(8,128)S(1)}, u32[]{:S(2)}, u32[]{:S(2)}) collective-permute-start(f32[64,4,256]{2,0,1:T(8,128)S(1)} %slice_bitcast_fusion.4), channel_id=1, source_target_pairs={{0,2},{1,3},{2,0},{3,1},{4,6},{5,7},{6,4},{7,5},{8,10},{9,11},{10,... | collective-permute-start | bytes 786440 | tf_op jit(solution)/shard_map/ppermute | solution.py:54
  215.0 16.0 %collective-permute-start.7 = (f32[64,4,256]{2,0,1:T(8,128)S(1)}, f32[64,4,256]{2,0,1:T(8,128)S(1)}, u32[]{:S(2)}, u32[]{:S(2)}) collective-permute-start(f32[64,4,256]{2,0,1:T(8,128)S(1)} %slice_bitcast_fusion.6), channel_id=1, source_target_pairs={{0,6},{1,7},{2,4},{3,5},{4,2},{5,3},{6,0},{7,1},{8,14},{9,15},{10,... | collective-permute-start | bytes 786440 | tf_op jit(solution)/shard_map/ppermute | solution.py:54
  225.6 9.6 %collective-permute-start.19 = (f32[64,4,256]{2,0,1:T(8,128)S(1)}, f32[64,4,256]{2,0,1:T(8,128)S(1)}, u32[]{:S(2)}, u32[]{:S(2)}) collective-permute-start(f32[64,4,256]{2,0,1:T(8,128)S(1)} %slice_bitcast_fusion), channel_id=1, source_target_pairs={{0,2},{1,3},{2,0},{3,1},{4,6},{5,7},{6,4},{7,5},{8,10},{9,11},{10,... | collective-permute-start | bytes 786440 | tf_op jit(solution)/shard_map/ppermute | solution.py:54
  226.4 8.8 %collective-permute-start.17 = (f32[64,4,256]{2,0,1:T(8,128)S(1)}, f32[64,4,256]{2,0,1:T(8,128)S(1)}, u32[]{:S(2)}, u32[]{:S(2)}) collective-permute-start(f32[64,4,256]{2,0,1:T(8,128)S(1)} %slice_bitcast_fusion.2), channel_id=1, source_target_pairs={{0,6},{1,7},{2,4},{3,5},{4,2},{5,3},{6,0},{7,1},{8,14},{9,15},{10,... | collective-permute-start | bytes 786440 | tf_op jit(solution)/shard_map/ppermute | solution.py:54
  231.1 8.7 %collective-permute-start.10 = (f32[2,64,2,256]{3,1,0,2:T(8,128)S(1)}, f32[2,64,2,256]{3,1,0,2:T(8,128)S(1)}, u32[]{:S(2)}, u32[]{:S(2)}) collective-permute-start(f32[2,64,2,256]{3,1,0,2:T(8,128)S(1)} %pad_maximum_fusion.19), channel_id=1, source_target_pairs={{0,8},{1,9},{2,10},{3,11},{4,12},{5,13},{6,14},{7,15},{8,0},{9,1},... | collective-permute-start | bytes 786440 | tf_op jit(solution)/shard_map/ppermute | solution.py:54
  235.4 10.7 %collective-permute-start.20 = (f32[2,64,2,256]{3,1,0,2:T(8,128)S(1)}, f32[2,64,2,256]{3,1,0,2:T(8,128)S(1)}, u32[]{:S(2)}, u32[]{:S(2)}) collective-permute-start(f32[2,64,2,256]{3,1,0,2:T(8,128)S(1)} %pad_maximum_fusion.20), channel_id=1, source_target_pairs={{0,8},{1,9},{2,10},{3,11},{4,12},{5,13},{6,14},{7,15},{8,0},{9,1},... | collective-permute-start | bytes 786440 | tf_op jit(solution)/shard_map/ppermute | solution.py:54
  239.9 18.0 %collective-permute-start.25 = (f32[2,64,256]{2,1,0:T(8,128)S(1)}, f32[2,64,256]{2,1,0:T(8,128)S(1)}, u32[]{:S(2)}, u32[]{:S(2)}) collective-permute-start(f32[2,64,256]{2,1,0:T(8,128)S(1)} %slice_bitcast_fusion.8), channel_id=1, source_target_pairs={{0,8},{1,9},{2,10},{3,11},{4,12},{5,13},{6,14},{7,15},{8,0},{9,1},... | collective-permute-start | bytes 393224 | tf_op jit(solution)/shard_map/ppermute | solution.py:54
  246.3 11.9 %collective-permute-start.21 = (f32[2,64,256]{2,1,0:T(8,128)S(1)}, f32[2,64,256]{2,1,0:T(8,128)S(1)}, u32[]{:S(2)}, u32[]{:S(2)}) collective-permute-start(f32[2,64,256]{2,1,0:T(8,128)S(1)} %get-tuple-element.76), channel_id=1, source_target_pairs={{0,0},{1,16},{2,32},{3,48},{4,64},{5,80},{6,96},{7,112},{8,8},{9,2... | collective-permute-start | bytes 393224 | tf_op jit(solution)/shard_map/ppermute | solution.py:54
  246.9 11.3 %collective-permute-start.22 = (f32[2,64,256]{2,1,0:T(8,128)S(1)}, f32[2,64,256]{2,1,0:T(8,128)S(1)}, u32[]{:S(2)}, u32[]{:S(2)}) collective-permute-start(f32[2,64,256]{2,1,0:T(8,128)S(1)} %get-tuple-element.78), channel_id=1, source_target_pairs={{0,1},{1,17},{2,33},{3,49},{4,65},{5,81},{6,97},{7,113},{8,9},{9,2... | collective-permute-start | bytes 393224 | tf_op jit(solution)/shard_map/ppermute | solution.py:54
  250.1 11.4 %collective-permute-start.23 = (f32[2,64,256]{2,1,0:T(8,128)S(1)}, f32[2,64,256]{2,1,0:T(8,128)S(1)}, u32[]{:S(2)}, u32[]{:S(2)}) collective-permute-start(f32[2,64,256]{2,1,0:T(8,128)S(1)} %get-tuple-element.79), channel_id=1, source_target_pairs={{0,4},{1,20},{2,36},{3,52},{4,68},{5,84},{6,100},{7,116},{8,12},{9... | collective-permute-start | bytes 393224 | tf_op jit(solution)/shard_map/ppermute | solution.py:54
  264.7 12.1 %collective-permute-start.27 = (f32[2,64,256]{2,1,0:T(8,128)S(1)}, f32[2,64,256]{2,1,0:T(8,128)S(1)}, u32[]{:S(2)}, u32[]{:S(2)}) collective-permute-start(f32[2,64,256]{2,1,0:T(8,128)S(1)} %select_multiply_fusion), channel_id=1, source_target_pairs={{0,96},{1,97},{2,98},{3,99},{4,100},{5,101},{6,102},{7,103},{8,104... | collective-permute-start | bytes 393224 | tf_op jit(solution)/shard_map/ppermute | solution.py:54
  271.3 7.9 %collective-permute-start.28 = (f32[2,64,256]{2,1,0:T(8,128)S(1)}, f32[2,64,256]{2,1,0:T(8,128)S(1)}, u32[]{:S(2)}, u32[]{:S(2)}) collective-permute-start(f32[2,64,256]{2,1,0:T(8,128)S(1)} %select_multiply_fusion), channel_id=1, source_target_pairs={{0,64},{1,65},{2,66},{3,67},{4,68},{5,69},{6,70},{7,71},{8,72},{9,... | collective-permute-start | bytes 393224 | tf_op jit(solution)/shard_map/ppermute | solution.py:54
  271.3 9.0 %collective-permute-start.29 = (f32[2,64,256]{2,1,0:T(8,128)S(1)}, f32[2,64,256]{2,1,0:T(8,128)S(1)}, u32[]{:S(2)}, u32[]{:S(2)}) collective-permute-start(f32[2,64,256]{2,1,0:T(8,128)S(1)} %select_multiply_fusion), channel_id=1, source_target_pairs={{0,32},{1,33},{2,34},{3,35},{4,36},{5,37},{6,38},{7,39},{8,40},{9,... | collective-permute-start | bytes 393224 | tf_op jit(solution)/shard_map/ppermute | solution.py:54
  272.8 8.9 %collective-permute-start.32 = (f32[256,256]{0,1:T(8,128)S(1)}, f32[256,256]{0,1:T(8,128)S(1)}, u32[]{:S(2)}, u32[]{:S(2)}) collective-permute-start(f32[256,256]{0,1:T(8,128)S(1)} %convolution_bitcast_fusion.1), channel_id=1, source_target_pairs={{0,1},{1,0},{2,3},{3,2},{4,5},{5,4},{6,7},{7,6},{8,9},{9,8},{10,11... | collective-permute-start | bytes 786440 | tf_op jit(solution)/shard_map/ppermute | solution.py:54
  281.6 11.8 %collective-permute-start.45 = (f32[512,256]{1,0:T(8,128)S(1)}, f32[512,256]{1,0:T(8,128)S(1)}, u32[]{:S(2)}, u32[]{:S(2)}) collective-permute-start(f32[512,256]{1,0:T(8,128)S(1)} %fusion.24), channel_id=1, source_target_pairs={{0,1},{1,0},{2,3},{3,2},{4,5},{5,4},{6,7},{7,6},{8,9},{9,8},{10,11... | collective-permute-start | bytes 1572872 | tf_op jit(solution)/shard_map/ppermute | solution.py:54
  281.8 8.8 %collective-permute-start.33 = (f32[256,256]{0,1:T(8,128)S(1)}, f32[256,256]{0,1:T(8,128)S(1)}, u32[]{:S(2)}, u32[]{:S(2)}) collective-permute-start(f32[256,256]{0,1:T(8,128)S(1)} %add.403), channel_id=1, source_target_pairs={{0,2},{1,3},{2,0},{3,1},{4,6},{5,7},{6,4},{7,5},{8,10},{9,11},{10,... | collective-permute-start | bytes 786440 | tf_op jit(solution)/shard_map/ppermute | solution.py:54
  290.6 10.0 %collective-permute-start.34 = (f32[256,256]{0,1:T(8,128)S(1)}, f32[256,256]{0,1:T(8,128)S(1)}, u32[]{:S(2)}, u32[]{:S(2)}) collective-permute-start(f32[256,256]{0,1:T(8,128)S(1)} %add.404), channel_id=1, source_target_pairs={{0,6},{1,7},{2,4},{3,5},{4,2},{5,3},{6,0},{7,1},{8,14},{9,15},{10,... | collective-permute-start | bytes 786440 | tf_op jit(solution)/shard_map/ppermute | solution.py:54
  291.9 21.5 %collective-permute-start.30 = (f32[512,256]{1,0:T(8,128)S(1)}, f32[512,256]{1,0:T(8,128)}, u32[]{:S(2)}, u32[]{:S(2)}) collective-permute-start(f32[512,256]{1,0:T(8,128)S(1)} %bitcast.191), channel_id=1, source_target_pairs={{0,0},{2,32},{4,64},{6,96},{8,8},{10,40},{12,72},{14,104},{17,17},... | collective-permute-start | bytes 1572872 | tf_op jit(solution)/shard_map/ppermute | solution.py:54
  293.5 20.1 %collective-permute-start.46 = (f32[512,256]{1,0:T(8,128)S(1)}, f32[512,256]{1,0:T(8,128)}, u32[]{:S(2)}, u32[]{:S(2)}) collective-permute-start(f32[512,256]{1,0:T(8,128)S(1)} %add.417), channel_id=1, source_target_pairs={{0,2},{1,3},{2,0},{3,1},{4,6},{5,7},{6,4},{7,5},{8,10},{9,11},{10,... | collective-permute-start | bytes 1572872 | tf_op jit(solution)/shard_map/ppermute | solution.py:54
  300.6 12.7 %collective-permute-start.35 = (f32[256,256]{0,1:T(8,128)S(1)}, f32[256,256]{0,1:T(8,128)S(1)}, u32[]{:S(2)}, u32[]{:S(2)}) collective-permute-start(f32[256,256]{0,1:T(8,128)S(1)} %add.405), channel_id=1, source_target_pairs={{0,32},{1,33},{2,34},{3,35},{4,36},{5,37},{6,38},{7,39},{8,40},{9,... | collective-permute-start | bytes 786440 | tf_op jit(solution)/shard_map/ppermute | solution.py:54
  313.3 9.5 %collective-permute-start.36 = (f32[256,256]{0,1:T(8,128)S(1)}, f32[256,256]{0,1:T(8,128)S(1)}, u32[]{:S(2)}, u32[]{:S(2)}) collective-permute-start(f32[256,256]{0,1:T(8,128)S(1)} %add.406), channel_id=1, source_target_pairs={{0,96},{1,97},{2,98},{3,99},{4,100},{5,101},{6,102},{7,103},{8,104... | collective-permute-start | bytes 786440 | tf_op jit(solution)/shard_map/ppermute | solution.py:54
  313.5 80.5 %collective-permute-start.31 = (f32[512,256]{1,0:T(8,128)}, f32[512,256]{1,0:T(8,128)}, u32[]{:S(2)}, u32[]{:S(2)}) collective-permute-start(f32[512,256]{1,0:T(8,128)} %collective-permute-done.30), channel_id=1, source_target_pairs={{0,1},{1,0},{2,3},{3,2},{4,5},{5,4},{6,7},{7,6},{8,9},{9,8},{10,11... | collective-permute-start | bytes 1572872 | tf_op jit(solution)/shard_map/ppermute | solution.py:54
  314.7 74.8 %collective-permute-start.47 = (f32[512,256]{1,0:T(8,128)S(1)}, f32[512,256]{1,0:T(8,128)}, u32[]{:S(2)}, u32[]{:S(2)}) collective-permute-start(f32[512,256]{1,0:T(8,128)S(1)} %add.418), channel_id=1, source_target_pairs={{0,6},{1,7},{2,4},{3,5},{4,2},{5,3},{6,0},{7,1},{8,14},{9,15},{10,... | collective-permute-start | bytes 1572872 | tf_op jit(solution)/shard_map/ppermute | solution.py:54
  387.2 9.0 %collective-permute-start.38 = (f32[256,256]{0,1:T(8,128)S(1)}, f32[256,256]{0,1:T(8,128)S(1)}, u32[]{:S(2)}, u32[]{:S(2)}) collective-permute-start(f32[256,256]{0,1:T(8,128)S(1)} %add.408), channel_id=1, source_target_pairs={{0,2},{1,3},{2,0},{3,1},{4,6},{5,7},{6,4},{7,5},{8,10},{9,11},{10,... | collective-permute-start | bytes 786440 | tf_op jit(solution)/shard_map/ppermute | solution.py:54
  390.6 16.5 %collective-permute-start.48 = (f32[512,256]{1,0:T(8,128)S(1)}, f32[512,256]{1,0:T(8,128)S(1)}, u32[]{:S(2)}, u32[]{:S(2)}) collective-permute-start(f32[512,256]{1,0:T(8,128)S(1)} %add.419), channel_id=1, source_target_pairs={{0,8},{1,9},{2,10},{3,11},{4,12},{5,13},{6,14},{7,15},{8,0},{9,1},... | collective-permute-start | bytes 1572872 | tf_op jit(solution)/shard_map/ppermute | solution.py:54
  396.1 7.9 %collective-permute-start.42 = (f32[256,256]{1,0:T(8,128)S(1)}, f32[256,256]{1,0:T(8,128)S(1)}, u32[]{:S(2)}, u32[]{:S(2)}) collective-permute-start(f32[256,256]{1,0:T(8,128)S(1)} %fusion.100), channel_id=1, source_target_pairs={{0,32},{1,33},{2,34},{3,35},{4,36},{5,37},{6,38},{7,39},{8,40},{9,... | collective-permute-start | bytes 786440 | tf_op jit(solution)/shard_map/ppermute | solution.py:54
  396.2 9.1 %collective-permute-start.39 = (f32[256,256]{0,1:T(8,128)S(1)}, f32[256,256]{0,1:T(8,128)S(1)}, u32[]{:S(2)}, u32[]{:S(2)}) collective-permute-start(f32[256,256]{0,1:T(8,128)S(1)} %add.409), channel_id=1, source_target_pairs={{0,6},{1,7},{2,4},{3,5},{4,2},{5,3},{6,0},{7,1},{8,14},{9,15},{10,... | collective-permute-start | bytes 786440 | tf_op jit(solution)/shard_map/ppermute | solution.py:54
  404.0 12.8 %collective-permute-start.43 = (f32[256,256]{1,0:T(8,128)S(1)}, f32[256,256]{1,0:T(8,128)S(1)}, u32[]{:S(2)}, u32[]{:S(2)}) collective-permute-start(f32[256,256]{1,0:T(8,128)S(1)} %add.413), channel_id=1, source_target_pairs={{0,96},{1,97},{2,98},{3,99},{4,100},{5,101},{6,102},{7,103},{8,104... | collective-permute-start | bytes 786440 | tf_op jit(solution)/shard_map/ppermute | solution.py:54
  405.3 9.3 %collective-permute-start.40 = (f32[256,256]{0,1:T(8,128)S(1)}, f32[256,256]{0,1:T(8,128)S(1)}, u32[]{:S(2)}, u32[]{:S(2)}) collective-permute-start(f32[256,256]{0,1:T(8,128)S(1)} %add.410), channel_id=1, source_target_pairs={{0,32},{1,33},{2,34},{3,35},{4,36},{5,37},{6,38},{7,39},{8,40},{9,... | collective-permute-start | bytes 786440 | tf_op jit(solution)/shard_map/ppermute | solution.py:54
  408.1 9.8 %collective-permute-start.49 = (f32[256,256]{1,0:T(8,128)S(1)}, f32[256,256]{1,0:T(8,128)S(1)}, u32[]{:S(2)}, u32[]{:S(2)}) collective-permute-start(f32[256,256]{1,0:T(8,128)S(1)} %fusion.35), channel_id=1, source_target_pairs={{0,32},{1,33},{2,34},{3,35},{4,36},{5,37},{6,38},{7,39},{8,40},{9,... | collective-permute-start | bytes 786440 | tf_op jit(solution)/shard_map/ppermute | solution.py:54
  414.7 9.4 %collective-permute-start.41 = (f32[256,256]{0,1:T(8,128)S(1)}, f32[256,256]{0,1:T(8,128)S(1)}, u32[]{:S(2)}, u32[]{:S(2)}) collective-permute-start(f32[256,256]{0,1:T(8,128)S(1)} %add.411), channel_id=1, source_target_pairs={{0,96},{1,97},{2,98},{3,99},{4,100},{5,101},{6,102},{7,103},{8,104... | collective-permute-start | bytes 786440 | tf_op jit(solution)/shard_map/ppermute | solution.py:54
  417.5 86.7 %collective-permute-start.44 = (f32[256,256]{1,0:T(8,128)}, f32[256,256]{1,0:T(8,128)}, u32[]{:S(2)}, u32[]{:S(2)}) collective-permute-start(f32[256,256]{1,0:T(8,128)} %add.414), channel_id=1, source_target_pairs={{0,16},{1,17},{2,18},{3,19},{4,20},{5,21},{6,22},{7,23},{8,24},{9,... | collective-permute-start | bytes 786440 | tf_op jit(solution)/shard_map/ppermute | solution.py:54
  418.6 76.0 %collective-permute-start.50 = (f32[256,256]{1,0:T(8,128)}, f32[256,256]{1,0:T(8,128)}, u32[]{:S(2)}, u32[]{:S(2)}) collective-permute-start(f32[256,256]{1,0:T(8,128)} %add.421), channel_id=1, source_target_pairs={{0,96},{1,97},{2,98},{3,99},{4,100},{5,101},{6,102},{7,103},{8,104... | collective-permute-start | bytes 786440 | tf_op jit(solution)/shard_map/ppermute | solution.py:54
  (19 other events, 149.5 us)
